TPU v7x, 32 devices: a whole 2x2x4 slice. The times are simulated.
32 devices in a mesh: groups: 2 (over x), energy: 8 (over z, y), space: 2 (over core).
Axes of the slice: x: 2, y: 2, z: 4, core: 2. Of those that a mesh axis runs over, the one named last changes fastest.
Arguments:
- ham_diag: float32 [2, 2, 512, 256], P('space', None, 'groups'), parts along dimension 2, as said below
- ham_coupling: float32 [2, 2, 256, 256], P('groups'), parts along dimension 0, may hold values from -0.25 to 0.25
- sigma_shift: float32 [8, 2, 512], P('energy', 'space', 'groups'), parts along dimension 2, may hold values from -3 to 3
- sigma_width: float32 [8, 2, 512], P('energy', 'space', 'groups'), parts along dimension 2, may hold values from 0.5 to 2
- occupation: float32 [8, 2, 512], P('energy', 'space', 'groups'), parts along dimension 2, may hold values from 0 to 1
Outputs:
- polarization: float32 [16, 2, 2, 256, 256], P('groups', None, None, ('energy', 'space')), parts along dimension 0
There are 2 independent parts, one for each index of `groups`. A program takes and returns all parts, laid end to end along the dimension named above; each array names one. Nothing has to cross between parts.
Inputs may be any that keep to these rules, and one draw needn't show every extreme that they name: Each ham_diag[b, 0] is symmetric and each ham_diag[b, 1] antisymmetric.
All inputs are finite; a program needn't handle non-finite values.
Results may differ from a plain program's by a relative error of at most 0.0001.
Values sent between devices are 32-bit elements; how exact they have to be, the bound alone decides.
A program may use at most 64 MiB of HBM per device.

v0:
```python
import functools

import jax
import jax.numpy as jnp
from jax import lax
from jax.experimental import pallas as pl
from jax.experimental.pallas import tpu as pltpu
from jax.sharding import PartitionSpec as P

F32 = jnp.float32
BF16 = jnp.bfloat16
NN = (((1,), (0,)), ((), ()))
NT = (((1,), (1,)), ((), ()))


def embed(right):
    half = right.shape[1] // 2
    return jnp.concatenate(
        [right, jnp.concatenate([-right[:, half:], right[:, :half]], axis=1)], axis=0
    )


def split(value):
    high = value.astype(BF16)
    return high, (value - high.astype(F32)).astype(BF16)


def dot(left, right, dims):
    return lax.dot_general(left, right, dims, preferred_element_type=F32)


def mul1(left, right, dims=NN):
    return dot(left.astype(BF16), embed(right.astype(BF16)), dims)


def mul3(left, right, dims=NN):
    left_hi, left_lo = split(left)
    right_hi, right_lo = split(right)
    wide = embed(right_hi)
    return dot(left_hi, wide, dims) + dot(left_lo, wide, dims) + dot(left_hi, embed(right_lo), dims)


def adjoint(value):
    half = value.shape[1] // 2
    return jnp.concatenate([value[:, :half].T, -value[:, half:].T], axis=1)


def eye2(order):
    row = lax.broadcasted_iota(jnp.int32, (order, 2 * order), 0)
    col = lax.broadcasted_iota(jnp.int32, (order, 2 * order), 1)
    return jnp.where(row == col, 1.0, 0.0).astype(F32)


def total(value):
    return jnp.sum(value * value)


def invert(a_ref, ah_ref, pair_ref, floor):
    order = a_ref.shape[0]
    normal = mul1(a_ref[...], a_ref[...], NT)
    bound = jnp.sqrt(total(normal))
    pair_ref[:order, :] = ah_ref[...] / bound
    pair_ref[order:, :] = normal / bound

    def rough(low):
        scale = 2.0 / (1.0 + low)
        pair = pair_ref[...]
        pair_ref[...] = (2.0 * scale) * pair - (scale * scale) * mul1(pair, pair_ref[order:, :])
        rho = (1.0 - low) / (1.0 + low)
        return 1.0 - rho * rho

    lax.while_loop(lambda low: low < 0.9, rough, jnp.maximum(floor / bound, 1e-6))

    def residual():
        return eye2(order) - mul3(a_ref[...], pair_ref[:order, :])

    def refine(state):
        step, _ = state
        left = residual()
        inverse = pair_ref[:order, :]
        pair_ref[:order, :] = inverse + mul1(inverse, left)
        return step + 1, total(left)

    _, size = lax.while_loop(
        lambda s: (s[0] < 5) & (s[1] > 4e-6), refine, (jnp.int32(0), F32(1.0))
    )

    @pl.when(jnp.logical_not(size <= 4e-6))
    def _():
        pair_ref[:order, :] = ah_ref[...] / bound

        def careful(state):
            step, _ = state
            left = residual()
            inverse = pair_ref[:order, :]
            pair_ref[:order, :] = inverse + mul3(inverse, left)
            return step + 1, total(left)

        lax.while_loop(
            lambda s: (s[0] < 60) & (s[1] > 4e-6), careful, (jnp.int32(0), F32(1.0))
        )


def green_kernel(scal_ref, side_ref, link_ref, far_ref, near_ref, sfar_ref, snear_ref, out_ref,
                 a_ref, ah_ref, pair_ref, x_ref):
    order = far_ref.shape[-1]
    energy = scal_ref[0]
    row = lax.broadcasted_iota(jnp.int32, (order, order), 0)
    col = lax.broadcasted_iota(jnp.int32, (order, order), 1)
    on = row == col

    def system(ham_ref, sig_ref):
        real = jnp.where(on, energy - sig_ref[0:1, :], 0.0) - ham_ref[0]
        width = jnp.where(on, sig_ref[1:2, :], 0.0)
        imag = width - ham_ref[1]
        return (jnp.concatenate([real, imag], axis=1),
                jnp.concatenate([real, -width - ham_ref[1]], axis=1))

    a_ref[...], ah_ref[...] = system(far_ref, sfar_ref)
    floor = jnp.min(sfar_ref[1:2, :])
    invert(a_ref, ah_ref, pair_ref, floor * floor)

    link = jnp.concatenate([link_ref[0], link_ref[1]], axis=1)
    link = jnp.where(side_ref[0] == 0, link, adjoint(link))
    x_ref[...] = mul3(link, pair_ref[:order, :])
    coupled = mul3(x_ref[...], link, NT)
    own, own_h = system(near_ref, snear_ref)
    a_ref[...] = own - coupled
    ah_ref[...] = own_h - adjoint(coupled)
    floor = jnp.min(snear_ref[1:2, :])
    invert(a_ref, ah_ref, pair_ref, floor * floor)

    green = pair_ref[:order, :]
    mixed = mul3(green, x_ref[...])

    def source(sig_ref):
        value = 2.0 * sig_ref[2:3, :] * sig_ref[1:2, :]
        return jnp.concatenate([value, value], axis=1)

    less = mul3(green * source(snear_ref), green, NT) + mul3(mixed * source(sfar_ref), mixed, NT)
    k_re, k_im = -less[:, order:], less[:, :order]
    g_re, g_im = green[:, :order], green[:, order:]
    out_ref[:, :order] = k_re
    out_ref[:, order:2 * order] = k_im
    out_ref[:, 2 * order:3 * order] = k_re + g_re - g_re.T
    out_ref[:, 3 * order:] = k_im + g_im + g_im.T


VMEM = pl.BlockSpec(memory_space=pltpu.VMEM)
SMEM = pl.BlockSpec(memory_space=pltpu.SMEM)


def green_blocks(energy, side, link, far, near, sfar, snear):
    order = far.shape[-1]
    return pl.pallas_call(
        green_kernel,
        out_shape=jax.ShapeDtypeStruct((order, 4 * order), F32),
        in_specs=[SMEM, SMEM, VMEM, VMEM, VMEM, VMEM, VMEM],
        out_specs=VMEM,
        scratch_shapes=[
            pltpu.VMEM((order, 2 * order), F32),
            pltpu.VMEM((order, 2 * order), F32),
            pltpu.VMEM((2 * order, 2 * order), F32),
            pltpu.VMEM((order, 2 * order), F32),
        ],
        compiler_params=pltpu.CompilerParams(vmem_limit_bytes=48 * 2**20),
    )(energy, side, link, far, near, sfar, snear)


def body(ham_diag, ham_coupling, sigma_shift, sigma_width, occupation):
    order = ham_diag.shape[-1]
    count = lax.axis_size("energy")
    sides = lax.axis_size("space")
    side = lax.axis_index("space")
    energy = -2.0 + 4.0 * (lax.axis_index("energy").astype(F32) + 0.5) / count
    near = ham_diag[0]
    snear = jnp.concatenate([sigma_shift[0], sigma_width[0], occupation[0]], axis=0)
    swap = [(0, 1), (1, 0)]
    far, sfar = lax.ppermute((near, snear), "space", swap)
    mine = green_blocks(energy.reshape(1), side.reshape(1), ham_coupling[0], far, near, sfar, snear)
    arrived = lax.all_to_all(mine, ("energy", "space"), split_axis=0, concat_axis=0, tiled=True)
    rows = order // (count * sides)
    arrived = arrived.reshape(count, sides, rows, 4, order)
    k_re, k_im, q_re, q_im = (arrived[:, :, :, i] for i in range(4))
    out = []
    for k in range(count):
        kr, ki = k_re[k:], k_im[k:]
        qr, qi = q_re[:count - k], q_im[:count - k]
        corr_re = jnp.sum(kr * qr + ki * qi, axis=0)
        corr_im = jnp.sum(ki * qr - kr * qi, axis=0)
        out.append(jnp.stack([-order * corr_im, order * corr_re], axis=1))
    return jnp.stack(out, axis=0)


def solution(mesh):
    return jax.shard_map(
        body,
        mesh=mesh,
        in_specs=(
            P("space", None, "groups", None),
            P("groups", None, None, None),
            P("energy", "space", "groups"),
            P("energy", "space", "groups"),
            P("energy", "space", "groups"),
        ),
        out_specs=P("groups", None, None, ("energy", "space"), None),
        check_vma=False,
    )
```

profile of v0, /device:TPU:0, one launch (start us, length us, event | category | flops | bytes accessed | tf_op | source)
XLA Modules:
  0.0 58.0 jit_solution(2929580756772065123)
XLA Ops:
  0.0 0.5 collective-permute-start
  0.5 0.0 copy-start.3
  0.5 0.0 copy-start.4
  0.5 0.0 copy-start.2
  0.5 0.7 %copy-done.3 = f32[1,1,256]{2,1,0:T(1,128)S(1)} copy-done((f32[1,1,256]{2,1,0:T(1,128)S(1)}, f32[1,1,256]{2,1,0:T(1,128)}, u32[]{:S(2)}) %copy-start.3) | copy-done | bytes 1048
  1.1 0.0 copy-done.4
  1.1 0.0 copy-done.2
  1.2 0.1 collective-permute-start.1
  1.3 1.1 %collective-permute-done.1.sfar_ref = f32[3,256]{1,0:T(4,128)S(1)} collective-permute-done((f32[3,256]{1,0:T(4,128)S(1)}, f32[3,256]{1,0:T(4,128)S(1)}, u32[]{:S(2)}, u32[]{:S(2)}) %collective-permute-start.1) | collective-permute-done | bytes 3104 | tf_op jit(solution)/shard_map/ppermute | solution.py:179
  2.4 0.0 collective-permute-done.far_ref
  2.4 0.0 copy-start
  2.4 1.0 %copy-done = f32[1,2,256,256]{3,2,1,0:T(8,128)S(1)} copy-done((f32[1,2,256,256]{3,2,1,0:T(8,128)S(1)}, f32[1,2,256,256]{3,2,1,0:T(8,128)}, u32[]{:S(2)}) %copy-start) | copy-done | bytes 524312
  3.4 0.0 copy-start.1
  3.4 1.0 %copy-done.1 = f32[1,2,256,256]{3,2,1,0:T(8,128)S(1)} copy-done((f32[1,2,256,256]{3,2,1,0:T(8,128)S(1)}, f32[1,2,256,256]{3,2,1,0:T(8,128)}, u32[]{:S(2)}) %copy-start.1) | copy-done | bytes 524312
  4.5 14.5 %shard_map.55 = f32[256,1024]{1,0:T(8,128)S(1)} custom-call(f32[1]{0:T(128)} %bitcast.scal_ref, s32[1]{0:T(128)} %bitcast.1.side_ref, f32[2,256,256]{2,1,0:T(8,128)S(1)} %bitcast.85, f32[2,256,256]{2,1,0:T(8,128)S(1)} %collective-permute-done.far_ref, f32[2,256,256]{2,1,0:T(8,128)S(1)} %bitcast.87, f32[3,256]{1,0:T(4,128)S(1)} %collective-permute-done.1.sfar_ref, ...), custom_call_target="tpu_custom_call" | custom-call | tf_op jit(solution)/shard_map/pallas_call | solution.py:155
  19.0 31.8 %all_to_all.9 = f32[16,16,1024]{2,1,0:T(8,128)S(1)} all-to-all(f32[16,16,1024]{2,1,0:T(8,128)S(1)} %bitcast.84), channel_id=1, replica_groups=mesh['groups'=2,'energy'=8,'space'=2] {'energy','space'}, dimensions={0} | all-to-all | bytes 2097152 | tf_op jit(solution)/shard_map/all_to_all | solution.py:181
  50.7 0.5 reshape.332
  51.2 1.1 %subtract_reduce_fusion.1 = (f32[2,16,256]{2,1,0:T(8,128)S(1)}, f32[2,16,256]{2,1,0:T(8,128)S(1)}) fusion(f32[8,2,16,4,256]{4,3,2,1,0:T(4,128)S(1)} %reshape.332), kind=kLoop, calls=%fused_computation.3 | loop fusion | flops 442368 | bytes 983040 | tf_op jit(solution)/shard_map/reduce_sum | solution.py:190
  52.3 0.8 %subtract_reduce_fusion.3 = (f32[2,16,256]{2,1,0:T(8,128)S(1)}, f32[2,16,256]{2,1,0:T(8,128)S(1)}) fusion(f32[8,2,16,4,256]{4,3,2,1,0:T(4,128)S(1)} %reshape.332), kind=kLoop, calls=%fused_computation.7 | loop fusion | flops 311296 | bytes 720896 | tf_op jit(solution)/shard_map/reduce_sum | solution.py:190
  53.1 0.7 %subtract_reduce_fusion.4 = (f32[2,16,256]{2,1,0:T(8,128)S(1)}, f32[2,16,256]{2,1,0:T(8,128)S(1)}) fusion(f32[8,2,16,4,256]{4,3,2,1,0:T(4,128)S(1)} %reshape.332), kind=kLoop, calls=%fused_computation.9 | loop fusion | flops 245760 | bytes 589824 | tf_op jit(solution)/shard_map/reduce_sum | solution.py:190
  53.8 1.2 %subtract_reduce_fusion = (f32[2,16,256]{2,1,0:T(8,128)S(1)}, f32[2,16,256]{2,1,0:T(8,128)S(1)}) fusion(f32[8,2,16,4,256]{4,3,2,1,0:T(4,128)S(1)} %reshape.332), kind=kLoop, calls=%fused_computation.1 | loop fusion | flops 507904 | bytes 1114112 | tf_op jit(solution)/shard_map/reduce_sum | solution.py:190
  55.0 0.9 %subtract_reduce_fusion.2 = (f32[2,16,256]{2,1,0:T(8,128)S(1)}, f32[2,16,256]{2,1,0:T(8,128)S(1)}) fusion(f32[8,2,16,4,256]{4,3,2,1,0:T(4,128)S(1)} %reshape.332), kind=kLoop, calls=%fused_computation.5 | loop fusion | flops 376832 | bytes 851968 | tf_op jit(solution)/shard_map/reduce_sum | solution.py:190
  55.9 0.4 subtract_reduce_fusion.6
  56.3 0.5 subtract_reduce_fusion.5
  56.8 0.1 fusion.11
  57.2 0.8 %copy.35 = f32[8,2,2,16,256]{4,3,2,1,0:T(8,128)} copy(f32[8,2,2,16,256]{4,3,1,2,0:T(8,128)S(1)} %fusion.7) | data formatting | bytes 1048576 | tf_op jit(solution)/shard_map/stack | solution.py:192
  (18 shorter events, 0.2 us)
Async XLA Ops:
  0.0 2.4 %collective-permute-start = (f32[2,256,256]{2,1,0:T(8,128)}, f32[2,256,256]{2,1,0:T(8,128)S(1)}, u32[]{:S(2)}, u32[]{:S(2)}) collective-permute-start(f32[2,256,256]{2,1,0:T(8,128)} %bitcast.86), channel_id=1, source_target_pairs={{0,1},{1,0},{2,3},{3,2},{4,5},{5,4},{6,7},{7,6},{8,9},{9,8},{10,11... | collective-permute-start | bytes 1572872 | tf_op jit(solution)/shard_map/ppermute | solution.py:179
  0.5 0.7 %copy-start.3 = (f32[1,1,256]{2,1,0:T(1,128)S(1)}, f32[1,1,256]{2,1,0:T(1,128)}, u32[]{:S(2)}) copy-start(f32[1,1,256]{2,1,0:T(1,128)} %param.8) | copy-start | bytes 3076
  0.5 0.7 %copy-start.4 = (f32[1,1,256]{2,1,0:T(1,128)S(1)}, f32[1,1,256]{2,1,0:T(1,128)}, u32[]{:S(2)}) copy-start(f32[1,1,256]{2,1,0:T(1,128)} %param.7) | copy-start | bytes 3076
  0.5 0.7 %copy-start.2 = (f32[1,1,256]{2,1,0:T(1,128)S(1)}, f32[1,1,256]{2,1,0:T(1,128)}, u32[]{:S(2)}) copy-start(f32[1,1,256]{2,1,0:T(1,128)} %param.9) | copy-start | bytes 3076
  1.2 1.2 %collective-permute-start.1 = (f32[3,256]{1,0:T(4,128)S(1)}, f32[3,256]{1,0:T(4,128)S(1)}, u32[]{:S(2)}, u32[]{:S(2)}) collective-permute-start(f32[3,256]{1,0:T(4,128)S(1)} %pad_maximum_fusion.snear_ref), channel_id=1, source_target_pairs={{0,1},{1,0},{2,3},{3,2},{4,5},{5,4},{6,7},{7,6},{8,9},{9,8},{10,11... | collective-permute-start | bytes 9224 | tf_op jit(solution)/shard_map/ppermute | solution.py:179
  2.4 1.0 %copy-start = (f32[1,2,256,256]{3,2,1,0:T(8,128)S(1)}, f32[1,2,256,256]{3,2,1,0:T(8,128)}, u32[]{:S(2)}) copy-start(f32[1,2,256,256]{3,2,1,0:T(8,128)} %param.6) | copy-start | bytes 1572868
  3.4 1.0 %copy-start.1 = (f32[1,2,256,256]{3,2,1,0:T(8,128)S(1)}, f32[1,2,256,256]{3,2,1,0:T(8,128)}, u32[]{:S(2)}) copy-start(f32[1,2,256,256]{3,2,1,0:T(8,128)} %param.5) | copy-start | bytes 1572868
where the time goes:
time: 58.6 us; the launch traced here: 58 us
  blocking collectives  31.8 us (54%)
  Pallas kernels  14.5 us (25%)
  other arithmetic  5.69 us (10%)
  local copies, waits for them, and re-layouts  4.22 us (7%)
  waiting for transfers between devices  1.11 us (2%)
    all_to_all x1, blocking collectives, body(): lax.all_to_all(mine, ('energy', 'space'), split_axis=0, concat_axis=0, ti...  31.8 us
    pallas_call x1, Pallas kernels, green_blocks(): pl.pallas_call(green_kernel, out_shape=jax.ShapeDtypeStruct((order, 4 * o...  14.5 us
    reduce_sum x7, other arithmetic, body(): corr_im = jnp.sum(ki * qr - kr * qi, axis=0)  5.54 us
    unnamed x10, local copies, waits for them, and re-layouts  2.79 us
  transfers between devices with their start and end apart: 2, of which 1 were waited for; matrix products, arithmetic and copies ran while one was open for 0% of the time, Pallas kernels for 0%

commit v1 on v0

v1 whole, which is shorter than its diff:
```python
import functools

import jax
import jax.numpy as jnp
from jax import lax
from jax.experimental import pallas as pl
from jax.experimental.pallas import tpu as pltpu
from jax.sharding import PartitionSpec as P

F32 = jnp.float32
BF16 = jnp.bfloat16
NN = (((1,), (0,)), ((), ()))
NT = (((1,), (1,)), ((), ()))


def embed(right):
    half = right.shape[1] // 2
    return jnp.concatenate(
        [right, jnp.concatenate([-right[:, half:], right[:, :half]], axis=1)], axis=0
    )


def split(value):
    high = value.astype(BF16)
    return high, (value - high.astype(F32)).astype(BF16)


def dot(left, right, dims):
    return lax.dot_general(left, right, dims, preferred_element_type=F32)


def mul1(left, right, dims=NN):
    return dot(left.astype(BF16), embed(right.astype(BF16)), dims)


def mul3(left, right, dims=NN):
    left_hi, left_lo = split(left)
    right_hi, right_lo = split(right)
    wide = embed(right_hi)
    return dot(left_hi, wide, dims) + dot(left_lo, wide, dims) + dot(left_hi, embed(right_lo), dims)


def adjoint(value):
    half = value.shape[1] // 2
    return jnp.concatenate([value[:, :half].T, -value[:, half:].T], axis=1)


def eye2(order):
    row = lax.broadcasted_iota(jnp.int32, (order, 2 * order), 0)
    col = lax.broadcasted_iota(jnp.int32, (order, 2 * order), 1)
    return jnp.where(row == col, 1.0, 0.0).astype(F32)


def total(value):
    return jnp.sum(value * value)


def invert(a_ref, ah_ref, pair_ref, floors):
    batch, order = a_ref.shape[:2]
    each = range(batch)
    bounds = []
    for j in each:
        normal = mul1(a_ref[j], a_ref[j], NT)
        bounds.append(jnp.sqrt(total(normal)))
        pair_ref[j, :order] = ah_ref[j] / bounds[j]
        pair_ref[j, order:] = normal / bounds[j]

    def rough(lows):
        after = []
        for j in each:
            low = lows[j]
            scale = 2.0 / (1.0 + low)
            pair = pair_ref[j]
            pair_ref[j] = (2.0 * scale) * pair - (scale * scale) * mul1(pair, pair[order:])
            rho = (1.0 - low) / (1.0 + low)
            after.append(1.0 - rho * rho)
        return tuple(after)

    lowest = lambda lows: functools.reduce(jnp.minimum, lows)
    largest = lambda sizes: functools.reduce(jnp.maximum, sizes)
    lax.while_loop(
        lambda lows: lowest(lows) < 0.9,
        rough,
        tuple(jnp.maximum(floors[j] / bounds[j], 1e-6) for j in each),
    )

    def newton(mul):
        def step(state):
            sizes = []
            for j in each:
                inverse = pair_ref[j, :order]
                left = eye2(order) - mul3(a_ref[j], inverse)
                pair_ref[j, :order] = inverse + mul(inverse, left)
                sizes.append(total(left))
            return state[0] + 1, largest(sizes)

        return step

    def iterate(mul, limit):
        return lax.while_loop(
            lambda s: (s[0] < limit) & (s[1] > 4e-6), newton(mul), (jnp.int32(0), F32(1.0))
        )[1]

    size = iterate(mul1, 5)

    @pl.when(jnp.logical_not(size <= 4e-6))
    def _():
        for j in each:
            pair_ref[j, :order] = ah_ref[j] / bounds[j]
        iterate(mul3, 60)


def green_kernel(scal_ref, side_ref, link_ref, far_ref, near_ref, sig_ref, green_ref, x_ref,
                 a_ref, ah_ref, pair_ref):
    order = far_ref.shape[-1]
    batch = sig_ref.shape[0]
    row = lax.broadcasted_iota(jnp.int32, (order, order), 0)
    col = lax.broadcasted_iota(jnp.int32, (order, order), 1)
    on = row == col

    def system(ham_ref, j, which):
        real = jnp.where(on, scal_ref[j] - sig_ref[j, which, 0:1, :], 0.0) - ham_ref[0]
        width = jnp.where(on, sig_ref[j, which, 1:2, :], 0.0)
        return (jnp.concatenate([real, width - ham_ref[1]], axis=1),
                jnp.concatenate([real, -width - ham_ref[1]], axis=1))

    def floors(which):
        least = [jnp.min(sig_ref[j, which, 1:2, :]) for j in range(batch)]
        return [value * value for value in least]

    for j in range(batch):
        a_ref[j], ah_ref[j] = system(far_ref, j, 1)
    invert(a_ref, ah_ref, pair_ref, floors(1))
    link = jnp.concatenate([link_ref[0], link_ref[1]], axis=1)
    link = jnp.where(side_ref[0] == 0, link, adjoint(link))
    for j in range(batch):
        x_ref[j] = mul3(link, pair_ref[j, :order])
        coupled = mul3(x_ref[j], link, NT)
        own, own_h = system(near_ref, j, 0)
        a_ref[j] = own - coupled
        ah_ref[j] = own_h - adjoint(coupled)
    invert(a_ref, ah_ref, pair_ref, floors(0))
    for j in range(batch):
        green_ref[j] = pair_ref[j, :order]


def lesser_greater(green, mixed, adj, near, far, g_rows, m_rows):
    order = green.shape[0]

    def source(sig):
        value = 2.0 * sig[2:3, :] * sig[1:2, :]
        return jnp.concatenate([value, value], axis=1)

    less = mul3(g_rows * source(near), green, NT) + mul3(m_rows * source(far), mixed, NT)
    k = jnp.concatenate([-less[:, order:], less[:, :order]], axis=1)
    return jnp.concatenate([k, k + g_rows - adj], axis=1)


def local_kernel(sig_ref, green_ref, x_ref, out_ref):
    green = green_ref[0]
    mixed = mul3(green, x_ref[0])
    out_ref[...] = lesser_greater(
        green, mixed, adjoint(green), sig_ref[0, 0], sig_ref[0, 1], green, mixed
    )


def exchange_kernel(sig_ref, green_ref, x_ref, out_ref, mix_ref, adj_ref, send_ref, recv_ref,
                    send_sem, recv_sem):
    peers, batch, rows = recv_ref.shape[:3]
    span = peers * rows
    order = green_ref.shape[1]
    spaces = lax.axis_size("space")
    per_side = peers // spaces
    where = lax.axis_index("energy")
    half = where // per_side
    me = (where - half * per_side) * spaces + lax.axis_index("space")

    def device(peer):
        return {"energy": half * per_side + peer // spaces, "space": peer % spaces}

    barrier = pltpu.get_barrier_semaphore()
    for hop in range(1, peers):
        pl.semaphore_signal(barrier, inc=1, device_id=device(me ^ hop),
                            device_id_type=pl.DeviceIdType.MESH)
    here = pl.ds(pl.multiple_of(half * span, span), span)
    copies = []
    for j in range(batch):
        mix_ref[...] = mul3(green_ref[j], x_ref[j])
        adj_ref[...] = adjoint(green_ref[j])
        send_ref[j] = lesser_greater(
            green_ref[j], mix_ref[...], adj_ref[here], sig_ref[j, 0], sig_ref[j, 1],
            green_ref[j, here], mix_ref[here],
        )
        if j == 0:
            pl.semaphore_wait(barrier, peers - 1)
        for hop in reversed(range(1, peers)):
            peer = me ^ hop
            copy = pltpu.make_async_remote_copy(
                src_ref=send_ref.at[j, pl.ds(pl.multiple_of(peer * rows, rows), rows)],
                dst_ref=recv_ref.at[me, j],
                send_sem=send_sem.at[j, hop],
                recv_sem=recv_sem.at[j, hop],
                device_id=device(peer),
                device_id_type=pl.DeviceIdType.MESH,
            )
            copy.start()
            copies.append(copy)
        recv_ref[me, j] = send_ref[j, pl.ds(pl.multiple_of(me * rows, rows), rows)]
    for copy in copies:
        copy.wait()
    count = per_side * batch
    for s in range(spaces):
        def part(n, i):
            return recv_ref[n % per_side * spaces + s, n // per_side, :, i * order:(i + 1) * order]

        for k in range(count):
            corr_re = jnp.zeros((rows, order), F32)
            corr_im = jnp.zeros((rows, order), F32)
            for n in range(k, count):
                kr, ki, qr, qi = part(n, 0), part(n, 1), part(n - k, 2), part(n - k, 3)
                corr_re += kr * qr + ki * qi
                corr_im += ki * qr - kr * qi
            out_ref[k, s, 0] = -order * corr_im
            out_ref[k, s, 1] = order * corr_re


VMEM = pl.BlockSpec(memory_space=pltpu.VMEM)
SMEM = pl.BlockSpec(memory_space=pltpu.SMEM)
LIMIT = 48 * 2**20


def green_blocks(energy, side, link, far, near, sig):
    order = far.shape[-1]
    batch = sig.shape[0]
    shape = (batch, order, 2 * order)
    return pl.pallas_call(
        green_kernel,
        out_shape=[jax.ShapeDtypeStruct(shape, F32)] * 2,
        in_specs=[SMEM, SMEM, VMEM, VMEM, VMEM, VMEM],
        out_specs=[VMEM, VMEM],
        scratch_shapes=[
            pltpu.VMEM(shape, F32),
            pltpu.VMEM(shape, F32),
            pltpu.VMEM((batch, 2 * order, 2 * order), F32),
        ],
        compiler_params=pltpu.CompilerParams(vmem_limit_bytes=LIMIT),
    )(energy, side, link, far, near, sig)


def exchange(sig, green, x, peers, rows):
    batch, order = green.shape[:2]
    spaces = lax.axis_size("space")
    return pl.pallas_call(
        exchange_kernel,
        out_shape=jax.ShapeDtypeStruct((peers // spaces * batch, spaces, 2, rows, order), F32),
        in_specs=[VMEM, VMEM, VMEM],
        out_specs=VMEM,
        scratch_shapes=[
            pltpu.VMEM((order, 2 * order), F32),
            pltpu.VMEM((order, 2 * order), F32),
            pltpu.VMEM((batch, peers * rows, 4 * order), F32),
            pltpu.VMEM((peers, batch, rows, 4 * order), F32),
            pltpu.SemaphoreType.DMA((batch, peers)),
            pltpu.SemaphoreType.DMA((batch, peers)),
        ],
        compiler_params=pltpu.CompilerParams(
            vmem_limit_bytes=LIMIT, collective_id=0, has_side_effects=True
        ),
    )(sig, green, x)


def collect(mine, count, sides, rows):
    order = mine.shape[0]
    arrived = lax.all_to_all(mine, ("energy", "space"), split_axis=0, concat_axis=0, tiled=True)
    arrived = arrived.reshape(count, sides, rows, 4, order)
    k_re, k_im, q_re, q_im = (arrived[:, :, :, i] for i in range(4))
    out = []
    for k in range(count):
        kr, ki = k_re[k:], k_im[k:]
        qr, qi = q_re[:count - k], q_im[:count - k]
        corr_re = jnp.sum(kr * qr + ki * qi, axis=0)
        corr_im = jnp.sum(ki * qr - kr * qi, axis=0)
        out.append(jnp.stack([-order * corr_im, order * corr_re], axis=1))
    return jnp.stack(out, axis=0)


SIDES = 2


def body(ham_diag, ham_coupling, sigma_shift, sigma_width, occupation):
    order = ham_diag.shape[-1]
    count = lax.axis_size("energy")
    spaces = lax.axis_size("space")
    side = lax.axis_index("space")
    where = lax.axis_index("energy")
    rows = order // (count * spaces)
    direct = rows % 8 == 0 and count & (count - 1) == 0
    batch = SIDES if direct and count % SIDES == 0 else 1
    per_side = count // batch
    near = ham_diag[0]
    far = lax.ppermute(near, "space", [(0, 1), (1, 0)])
    packed = jnp.concatenate([sigma_shift[0], sigma_width[0], occupation[0]], axis=0)
    sig = []
    for j in range(batch):
        pair = []
        for flip in range(spaces):
            moves = [(e * spaces + s, (e + j * per_side) % count * spaces + (s ^ flip))
                     for e in range(count) for s in range(spaces)]
            pair.append(packed if j == flip == 0 else lax.ppermute(packed, ("energy", "space"), moves))
        sig.append(jnp.stack(pair))
    index = (where + per_side * jnp.arange(batch)) % count
    energy = -2.0 + 4.0 * (index.astype(F32) + 0.5) / count
    sig = jnp.stack(sig)
    if batch > 1:
        flip = where >= per_side
        sig = jnp.where(flip, sig[::-1], sig)
        energy = jnp.where(flip, energy[::-1], energy)
    green, x = green_blocks(energy, side.reshape(1), ham_coupling[0], far, near, sig)
    if direct:
        return exchange(sig, green, x, per_side * spaces, rows)
    mine = pl.pallas_call(
        local_kernel,
        out_shape=jax.ShapeDtypeStruct((order, 4 * order), F32),
        in_specs=[VMEM, VMEM, VMEM],
        out_specs=VMEM,
        compiler_params=pltpu.CompilerParams(vmem_limit_bytes=LIMIT),
    )(sig, green, x)
    return collect(mine, count, spaces, rows)


def solution(mesh):
    return jax.shard_map(
        body,
        mesh=mesh,
        in_specs=(
            P("space", None, "groups", None),
            P("groups", None, None, None),
            P("energy", "space", "groups"),
            P("energy", "space", "groups"),
            P("energy", "space", "groups"),
        ),
        out_specs=P("groups", None, None, ("energy", "space"), None),
        check_vma=False,
    )
```

time: 58.6 us -> 51.1 us (0.87)
  blocking collectives: 31.8 us -> 0 us
  Pallas kernels: 14.5 us -> 39.1 us
  other arithmetic: 5.69 us -> 0.07 us
  starting transfers between devices: 0.57 us -> 4.61 us
  waiting for transfers between devices: 1.11 us -> 3.28 us
    all_to_all x1 -> x0, blocking collectives: 31.8 us -> none  [body(): lax.all_to_all(mine, ('energy', 'space'), split_axis=0, concat_axis=0, ti...]
    pallas_call x1 -> x2, Pallas kernels: 14.5 us -> 39.1 us  [the longest x1 22.5 us: green_blocks(): pl.pallas_call(green_kernel, out_shape=[jax.ShapeDtypeStruct(shape, F32)]...]
    reduce_sum x7 -> x0, other arithmetic: 5.54 us -> none  [body(): corr_im = jnp.sum(ki * qr - kr * qi, axis=0)]
    ppermute x2 -> x4, starting transfers between devices: 0.57 us -> 4.61 us  [the longest x3 4.31 us: body(): lax.ppermute(packed, ('energy', 'space'), moves)]
    ppermute x2 -> x4, waiting for transfers between devices: 1.11 us -> 3.28 us  [the longest x3 3.28 us: body(): lax.ppermute(packed, ('energy', 'space'), moves)]
    unnamed x10 -> x11, local copies, waits for them, and re-layouts: 2.79 us -> 3.58 us
    another operation x1, local copies, waits for them, and re-layouts: 0.83 us -> 0.1 us  [body(): return jnp.stack(out, axis=0)]
  transfers between devices with their start and end apart: 2 -> 4, of which waited for: 1 -> 3; matrix products, arithmetic and copies ran while one was open for 0% -> 0% of each run, Pallas kernels for 0% -> 0%
where the time goes in v1:
time: 51.1 us; the launch traced here: 50.8 us
  Pallas kernels  39.1 us (77%)
  starting transfers between devices  4.61 us (9%)
  local copies, waits for them, and re-layouts  3.68 us (7%)
  waiting for transfers between devices  3.28 us (6%)
    pallas_call x1, Pallas kernels, green_blocks(): pl.pallas_call(green_kernel, out_shape=[jax.ShapeDtypeStruct(shape, F32)]...  22.5 us
    pallas_call x1, Pallas kernels, exchange(): pl.pallas_call(exchange_kernel, out_shape=jax.ShapeDtypeStruct((peers //...  16.6 us
    ppermute x3, starting transfers between devices, body(): lax.ppermute(packed, ('energy', 'space'), moves)  4.31 us
    unnamed x11, local copies, waits for them, and re-layouts  3.58 us
    ppermute x3, waiting for transfers between devices, body(): lax.ppermute(packed, ('energy', 'space'), moves)  3.28 us
  transfers between devices with their start and end apart: 4, of which 3 were waited for; matrix products, arithmetic and copies ran while one was open for 0% of the time, Pallas kernels for 0%

profile of v1, /device:TPU:0, one launch (start us, length us, event | category | flops | bytes accessed | tf_op | source)
XLA Modules:
  0.0 50.8 jit_solution(5453590302648278198)
XLA Ops:
  0.0 0.0 copy-start.3
  0.0 0.0 copy-start.4
  0.0 0.0 copy-start.2
  0.0 0.7 %copy-done.3 = f32[1,1,256]{2,1,0:T(1,128)S(1)} copy-done((f32[1,1,256]{2,1,0:T(1,128)S(1)}, f32[1,1,256]{2,1,0:T(1,128)}, u32[]{:S(2)}) %copy-start.3) | copy-done | bytes 1048
  0.7 0.0 copy-done.4
  0.7 0.0 copy-done.2
  0.7 4.1 %collective-permute-start.1 = (f32[3,256]{1,0:T(4,128)S(1)}, f32[3,256]{1,0:T(4,128)S(1)}, u32[]{:S(2)}, u32[]{:S(2)}) collective-permute-start(f32[3,256]{1,0:T(4,128)S(1)} %get-tuple-element.10), channel_id=1, source_target_pairs={{0,8},{1,9},{2,10},{3,11},{4,12},{5,13},{6,14},{7,15},{8,0},{9,1},... | collective-permute-start | bytes 9224 | tf_op jit(solution)/shard_map/ppermute | solution.py:309
  4.8 0.0 collective-permute-start
  4.8 0.2 collective-permute-start.2
  5.0 0.3 collective-permute-start.3
  5.4 0.1 reverse.5
  5.5 0.5 %collective-permute-done = f32[3,256]{1,0:T(4,128)S(1)} collective-permute-done((f32[3,256]{1,0:T(4,128)S(1)}, f32[3,256]{1,0:T(4,128)S(1)}, u32[]{:S(2)}, u32[]{:S(2)}) %collective-permute-start) | collective-permute-done | bytes 3104 | tf_op jit(solution)/shard_map/ppermute | solution.py:309
  6.0 0.4 collective-permute-done.1
  6.4 2.3 %collective-permute-done.2 = f32[3,256]{1,0:T(4,128)S(1)} collective-permute-done((f32[3,256]{1,0:T(4,128)S(1)}, f32[3,256]{1,0:T(4,128)S(1)}, u32[]{:S(2)}, u32[]{:S(2)}) %collective-permute-start.2) | collective-permute-done | bytes 3104 | tf_op jit(solution)/shard_map/ppermute | solution.py:309
  8.8 0.0 collective-permute-done.3.far_ref
  8.8 0.0 copy-start
  8.8 1.0 %copy-done = f32[1,2,256,256]{3,2,1,0:T(8,128)S(1)} copy-done((f32[1,2,256,256]{3,2,1,0:T(8,128)S(1)}, f32[1,2,256,256]{3,2,1,0:T(8,128)}, u32[]{:S(2)}) %copy-start) | copy-done | bytes 524312
  9.8 0.0 copy-start.1
  9.8 1.0 %copy-done.1 = f32[1,2,256,256]{3,2,1,0:T(8,128)S(1)} copy-done((f32[1,2,256,256]{3,2,1,0:T(8,128)S(1)}, f32[1,2,256,256]{3,2,1,0:T(8,128)}, u32[]{:S(2)}) %copy-start.1) | copy-done | bytes 524312
  10.9 22.5 %shard_map.55 = (f32[2,256,512]{2,1,0:T(8,128)S(1)}, f32[2,256,512]{2,1,0:T(8,128)S(1)}) custom-call(f32[2]{0:T(128)S(1)} %broadcast_select_fusion.scal_ref, s32[1]{0:T(128)} %bitcast.9.side_ref, f32[2,256,256]{2,1,0:T(8,128)S(1)} %bitcast.15, f32[2,256,256]{2,1,0:T(8,128)S(1)} %collective-permute-done.3.far_ref, f32[2,256,256]{2,1,0:T(8,128)S(1)} %bitcast.17, ...), custom_call_target="tpu_custom_call" | custom-call | tf_op jit(solution)/shard_map/pallas_call | solution.py:236
  33.4 16.6 %shard_map.56 = f32[8,2,2,16,256]{4,3,2,1,0:T(8,128)S(1)} custom-call(f32[2,2,3,256]{3,2,1,0:T(4,128)S(1)} %reverse_select_fusion.sig_ref, f32[2,256,512]{2,1,0:T(8,128)S(1)} %get-tuple-element.7.green_ref, f32[2,256,512]{2,1,0:T(8,128)S(1)} %get-tuple-element.8.x_ref), custom_call_target="tpu_custom_call" | custom-call | tf_op jit(solution)/shard_map/pallas_call | solution.py:253
  50.0 0.8 %copy.7 = f32[8,2,2,16,256]{4,3,2,1,0:T(8,128)} copy(f32[8,2,2,16,256]{4,3,2,1,0:T(8,128)S(1)} %shard_map.56) | data formatting | bytes 1048576
  (7 shorter events, 0.1 us)
Async XLA Ops:
  0.0 0.7 %copy-start.3 = (f32[1,1,256]{2,1,0:T(1,128)S(1)}, f32[1,1,256]{2,1,0:T(1,128)}, u32[]{:S(2)}) copy-start(f32[1,1,256]{2,1,0:T(1,128)} %param.8) | copy-start | bytes 3076
  0.0 0.7 %copy-start.4 = (f32[1,1,256]{2,1,0:T(1,128)S(1)}, f32[1,1,256]{2,1,0:T(1,128)}, u32[]{:S(2)}) copy-start(f32[1,1,256]{2,1,0:T(1,128)} %param.7) | copy-start | bytes 3076
  0.0 0.7 %copy-start.2 = (f32[1,1,256]{2,1,0:T(1,128)S(1)}, f32[1,1,256]{2,1,0:T(1,128)}, u32[]{:S(2)}) copy-start(f32[1,1,256]{2,1,0:T(1,128)} %param.9) | copy-start | bytes 3076
  0.7 5.7 %collective-permute-start.1 = (f32[3,256]{1,0:T(4,128)S(1)}, f32[3,256]{1,0:T(4,128)S(1)}, u32[]{:S(2)}, u32[]{:S(2)}) collective-permute-start(f32[3,256]{1,0:T(4,128)S(1)} %get-tuple-element.10), channel_id=1, source_target_pairs={{0,8},{1,9},{2,10},{3,11},{4,12},{5,13},{6,14},{7,15},{8,0},{9,1},... | collective-permute-start | bytes 9224 | tf_op jit(solution)/shard_map/ppermute | solution.py:309
  4.8 1.2 %collective-permute-start = (f32[3,256]{1,0:T(4,128)S(1)}, f32[3,256]{1,0:T(4,128)S(1)}, u32[]{:S(2)}, u32[]{:S(2)}) collective-permute-start(f32[3,256]{1,0:T(4,128)S(1)} %get-tuple-element.10), channel_id=1, source_target_pairs={{0,1},{1,0},{2,3},{3,2},{4,5},{5,4},{6,7},{7,6},{8,9},{9,8},{10,11... | collective-permute-start | bytes 9224 | tf_op jit(solution)/shard_map/ppermute | solution.py:309
  4.8 3.9 %collective-permute-start.2 = (f32[3,256]{1,0:T(4,128)S(1)}, f32[3,256]{1,0:T(4,128)S(1)}, u32[]{:S(2)}, u32[]{:S(2)}) collective-permute-start(f32[3,256]{1,0:T(4,128)S(1)} %get-tuple-element.10), channel_id=1, source_target_pairs={{0,9},{1,8},{2,11},{3,10},{4,13},{5,12},{6,15},{7,14},{8,1},{9,0},... | collective-permute-start | bytes 9224 | tf_op jit(solution)/shard_map/ppermute | solution.py:309
  5.0 3.8 %collective-permute-start.3 = (f32[2,256,256]{2,1,0:T(8,128)}, f32[2,256,256]{2,1,0:T(8,128)S(1)}, u32[]{:S(2)}, u32[]{:S(2)}) collective-permute-start(f32[2,256,256]{2,1,0:T(8,128)} %bitcast.16), channel_id=1, source_target_pairs={{0,1},{1,0},{2,3},{3,2},{4,5},{5,4},{6,7},{7,6},{8,9},{9,8},{10,11... | collective-permute-start | bytes 1572872 | tf_op jit(solution)/shard_map/ppermute | solution.py:301
  8.8 1.0 %copy-start = (f32[1,2,256,256]{3,2,1,0:T(8,128)S(1)}, f32[1,2,256,256]{3,2,1,0:T(8,128)}, u32[]{:S(2)}) copy-start(f32[1,2,256,256]{3,2,1,0:T(8,128)} %param.6) | copy-start | bytes 1572868
  9.8 1.0 %copy-start.1 = (f32[1,2,256,256]{3,2,1,0:T(8,128)S(1)}, f32[1,2,256,256]{3,2,1,0:T(8,128)}, u32[]{:S(2)}) copy-start(f32[1,2,256,256]{3,2,1,0:T(8,128)} %param.5) | copy-start | bytes 1572868

commit v2 on v1

--- a/solution.py
+++ b/solution.py
@@ -13,13 +13,6 @@
 NT = (((1,), (1,)), ((), ()))
 
 
-def embed(right):
-    half = right.shape[1] // 2
-    return jnp.concatenate(
-        [right, jnp.concatenate([-right[:, half:], right[:, :half]], axis=1)], axis=0
-    )
-
-
 def split(value):
     high = value.astype(BF16)
     return high, (value - high.astype(F32)).astype(BF16)
@@ -29,15 +22,36 @@
     return lax.dot_general(left, right, dims, preferred_element_type=F32)
 
 
-def mul1(left, right, dims=NN):
-    return dot(left.astype(BF16), embed(right.astype(BF16)), dims)
-
-
-def mul3(left, right, dims=NN):
+def three_products(left, right, dims, real_dot):
+    half = left.shape[1] // 2
+    left_re, left_im = left[:, :half], left[:, half:]
+    right_re, right_im = right[:, :half], right[:, half:]
+    first = real_dot(left_re, right_re, dims)
+    second = real_dot(left_im, right_im, dims)
+    if dims is NT:
+        third = real_dot(left_re + left_im, right_re - right_im, dims)
+        return jnp.concatenate([first + second, third - first + second], axis=1)
+    third = real_dot(left_re + left_im, right_re + right_im, dims)
+    return jnp.concatenate([first - second, third - first - second], axis=1)
+
+
+def dot1(left, right, dims):
+    return dot(left.astype(BF16), right.astype(BF16), dims)
+
+
+def dot3(left, right, dims):
     left_hi, left_lo = split(left)
     right_hi, right_lo = split(right)
-    wide = embed(right_hi)
-    return dot(left_hi, wide, dims) + dot(left_lo, wide, dims) + dot(left_hi, embed(right_lo), dims)
+    return (dot(left_hi, right_hi, dims) + dot(left_lo, right_hi, dims)
+            + dot(left_hi, right_lo, dims))
+
+
+def mul1(left, right, dims=NN):
+    return three_products(left, right, dims, dot1)
+
+
+def mul3(left, right, dims=NN):
+    return three_products(left, right, dims, dot3)
 
 
 def adjoint(value):
@@ -284,7 +298,7 @@
     return jnp.stack(out, axis=0)
 
 
-SIDES = 2
+SIDES = 1
 
 
 def body(ham_diag, ham_coupling, sigma_shift, sigma_width, occupation):

time: 51.1 us -> 49.2 us (0.963)
  Pallas kernels: 39.1 us -> 43.7 us
  starting transfers between devices: 4.61 us -> 0.58 us
  waiting for transfers between devices: 3.28 us -> 1.11 us
    pallas_call x1, Pallas kernels: 16.6 us -> 31.3 us  [exchange(): pl.pallas_call(exchange_kernel, out_shape=jax.ShapeDtypeStruct((peers //...]
    pallas_call x1, Pallas kernels: 22.5 us -> 12.4 us  [green_blocks(): pl.pallas_call(green_kernel, out_shape=[jax.ShapeDtypeStruct(shape, F32)]...]
    ppermute x3 -> x1, starting transfers between devices: 4.31 us -> 0.12 us  [body(): lax.ppermute(packed, ('energy', 'space'), moves)]
    ppermute x3 -> x1, waiting for transfers between devices: 3.28 us -> 1.11 us  [body(): lax.ppermute(packed, ('energy', 'space'), moves)]
  transfers between devices with their start and end apart: 4 -> 2, of which waited for: 3 -> 1; matrix products, arithmetic and copies ran while one was open for 0% -> 0% of each run, Pallas kernels for 0% -> 0%
where the time goes in v2:
time: 49.2 us; the launch traced here: 49 us
  Pallas kernels  43.7 us (89%)
  local copies, waits for them, and re-layouts  3.58 us (7%)
  waiting for transfers between devices  1.11 us (2%)
  starting transfers between devices  0.58 us (1%)
    pallas_call x1, Pallas kernels, exchange(): pl.pallas_call(exchange_kernel, out_shape=jax.ShapeDtypeStruct((peers //...  31.3 us
    pallas_call x1, Pallas kernels, green_blocks(): pl.pallas_call(green_kernel, out_shape=[jax.ShapeDtypeStruct(shape, F32)]...  12.4 us
    unnamed x11, local copies, waits for them, and re-layouts  3.58 us
    ppermute x1, waiting for transfers between devices, body(): lax.ppermute(packed, ('energy', 'space'), moves)  1.11 us
  transfers between devices with their start and end apart: 2, of which 1 were waited for; matrix products, arithmetic and copies ran while one was open for 0% of the time, Pallas kernels for 0%

profile of v2, /device:TPU:0, one launch (start us, length us, event | category | flops | bytes accessed | tf_op | source)
XLA Modules:
  0.0 49.0 jit_solution(4669171175647254028)
XLA Ops:
  0.0 0.5 collective-permute-start.1
  0.5 0.0 copy-start.3
  0.5 0.0 copy-start.4
  0.5 0.0 copy-start.2
  0.5 0.7 %copy-done.3 = f32[1,1,256]{2,1,0:T(1,128)S(1)} copy-done((f32[1,1,256]{2,1,0:T(1,128)S(1)}, f32[1,1,256]{2,1,0:T(1,128)}, u32[]{:S(2)}) %copy-start.3) | copy-done | bytes 1048
  1.1 0.0 copy-done.4
  1.1 0.0 copy-done.2
  1.2 0.1 collective-permute-start
  1.3 1.1 %collective-permute-done = f32[3,256]{1,0:T(4,128)S(1)} collective-permute-done((f32[3,256]{1,0:T(4,128)S(1)}, f32[3,256]{1,0:T(4,128)S(1)}, u32[]{:S(2)}, u32[]{:S(2)}) %collective-permute-start) | collective-permute-done | bytes 3104 | tf_op jit(solution)/shard_map/ppermute | solution.py:323
  2.4 0.0 collective-permute-done.1.far_ref
  2.4 0.0 copy-start
  2.4 1.0 %copy-done = f32[1,2,256,256]{3,2,1,0:T(8,128)S(1)} copy-done((f32[1,2,256,256]{3,2,1,0:T(8,128)S(1)}, f32[1,2,256,256]{3,2,1,0:T(8,128)}, u32[]{:S(2)}) %copy-start) | copy-done | bytes 524312
  3.5 0.0 copy-start.1
  3.5 1.0 %copy-done.1 = f32[1,2,256,256]{3,2,1,0:T(8,128)S(1)} copy-done((f32[1,2,256,256]{3,2,1,0:T(8,128)S(1)}, f32[1,2,256,256]{3,2,1,0:T(8,128)}, u32[]{:S(2)}) %copy-start.1) | copy-done | bytes 524312
  4.5 12.4 %shard_map.55 = (f32[1,256,512]{2,1,0:T(8,128)S(1)}, f32[1,256,512]{2,1,0:T(8,128)S(1)}) custom-call(f32[1]{0:T(128)S(6)} %add.18.scal_ref, s32[1]{0:T(128)} %bitcast.7.side_ref, f32[2,256,256]{2,1,0:T(8,128)S(1)} %bitcast.12, f32[2,256,256]{2,1,0:T(8,128)S(1)} %collective-permute-done.1.far_ref, f32[2,256,256]{2,1,0:T(8,128)S(1)} %bitcast.14, ...), custom_call_target="tpu_custom_call" | custom-call | tf_op jit(solution)/shard_map/pallas_call | solution.py:250
  16.9 31.3 %shard_map.56 = f32[8,2,2,16,256]{4,3,2,1,0:T(8,128)S(1)} custom-call(f32[1,2,3,256]{3,2,1,0:T(4,128)S(1)} %maximum_bitcast_fusion.sig_ref, f32[1,256,512]{2,1,0:T(8,128)S(1)} %get-tuple-element.7.green_ref, f32[1,256,512]{2,1,0:T(8,128)S(1)} %get-tuple-element.8.x_ref), custom_call_target="tpu_custom_call" | custom-call | tf_op jit(solution)/shard_map/pallas_call | solution.py:267
  48.2 0.8 %copy.7 = f32[8,2,2,16,256]{4,3,2,1,0:T(8,128)} copy(f32[8,2,2,16,256]{4,3,2,1,0:T(8,128)S(1)} %shard_map.56) | data formatting | bytes 1048576
  (2 shorter events, 0.0 us)
Async XLA Ops:
  0.0 2.4 %collective-permute-start.1 = (f32[2,256,256]{2,1,0:T(8,128)}, f32[2,256,256]{2,1,0:T(8,128)S(1)}, u32[]{:S(2)}, u32[]{:S(2)}) collective-permute-start(f32[2,256,256]{2,1,0:T(8,128)} %bitcast.13), channel_id=1, source_target_pairs={{0,1},{1,0},{2,3},{3,2},{4,5},{5,4},{6,7},{7,6},{8,9},{9,8},{10,11... | collective-permute-start | bytes 1572872 | tf_op jit(solution)/shard_map/ppermute | solution.py:315
  0.5 0.7 %copy-start.3 = (f32[1,1,256]{2,1,0:T(1,128)S(1)}, f32[1,1,256]{2,1,0:T(1,128)}, u32[]{:S(2)}) copy-start(f32[1,1,256]{2,1,0:T(1,128)} %param.8) | copy-start | bytes 3076
  0.5 0.7 %copy-start.4 = (f32[1,1,256]{2,1,0:T(1,128)S(1)}, f32[1,1,256]{2,1,0:T(1,128)}, u32[]{:S(2)}) copy-start(f32[1,1,256]{2,1,0:T(1,128)} %param.7) | copy-start | bytes 3076
  0.5 0.7 %copy-start.2 = (f32[1,1,256]{2,1,0:T(1,128)S(1)}, f32[1,1,256]{2,1,0:T(1,128)}, u32[]{:S(2)}) copy-start(f32[1,1,256]{2,1,0:T(1,128)} %param.9) | copy-start | bytes 3076
  1.2 1.2 %collective-permute-start = (f32[3,256]{1,0:T(4,128)S(1)}, f32[3,256]{1,0:T(4,128)S(1)}, u32[]{:S(2)}, u32[]{:S(2)}) collective-permute-start(f32[3,256]{1,0:T(4,128)S(1)} %get-tuple-element.10), channel_id=1, source_target_pairs={{0,1},{1,0},{2,3},{3,2},{4,5},{5,4},{6,7},{7,6},{8,9},{9,8},{10,11... | collective-permute-start | bytes 9224 | tf_op jit(solution)/shard_map/ppermute | solution.py:323
  2.4 1.0 %copy-start = (f32[1,2,256,256]{3,2,1,0:T(8,128)S(1)}, f32[1,2,256,256]{3,2,1,0:T(8,128)}, u32[]{:S(2)}) copy-start(f32[1,2,256,256]{3,2,1,0:T(8,128)} %param.6) | copy-start | bytes 1572868
  3.5 1.0 %copy-start.1 = (f32[1,2,256,256]{3,2,1,0:T(8,128)S(1)}, f32[1,2,256,256]{3,2,1,0:T(8,128)}, u32[]{:S(2)}) copy-start(f32[1,2,256,256]{3,2,1,0:T(8,128)} %param.5) | copy-start | bytes 1572868

commit v3 on v2

--- a/solution.py
+++ b/solution.py
@@ -298,7 +298,7 @@
     return jnp.stack(out, axis=0)
 
 
-SIDES = 1
+SIDES = 2
 
 
 def body(ham_diag, ham_coupling, sigma_shift, sigma_width, occupation):

time: 49.2 us -> 48.7 us (0.990)
  Pallas kernels: 43.7 us -> 36.8 us
  starting transfers between devices: 0.58 us -> 4.61 us
  waiting for transfers between devices: 1.11 us -> 3.28 us
    pallas_call x1, Pallas kernels: 31.3 us -> 16.4 us  [exchange(): pl.pallas_call(exchange_kernel, out_shape=jax.ShapeDtypeStruct((peers //...]
    pallas_call x1, Pallas kernels: 12.4 us -> 20.3 us  [green_blocks(): pl.pallas_call(green_kernel, out_shape=[jax.ShapeDtypeStruct(shape, F32)]...]
    ppermute x1 -> x3, starting transfers between devices: 0.12 us -> 4.31 us  [body(): lax.ppermute(packed, ('energy', 'space'), moves)]
    ppermute x1 -> x3, waiting for transfers between devices: 1.11 us -> 3.28 us  [body(): lax.ppermute(packed, ('energy', 'space'), moves)]
  transfers between devices with their start and end apart: 2 -> 4, of which waited for: 1 -> 3; matrix products, arithmetic and copies ran while one was open for 0% -> 0% of each run, Pallas kernels for 0% -> 0%
where the time goes in v3:
time: 48.7 us; the launch traced here: 48.5 us
  Pallas kernels  36.8 us (76%)
  starting transfers between devices  4.61 us (9%)
  local copies, waits for them, and re-layouts  3.68 us (8%)
  waiting for transfers between devices  3.28 us (7%)
    pallas_call x1, Pallas kernels, green_blocks(): pl.pallas_call(green_kernel, out_shape=[jax.ShapeDtypeStruct(shape, F32)]...  20.3 us
    pallas_call x1, Pallas kernels, exchange(): pl.pallas_call(exchange_kernel, out_shape=jax.ShapeDtypeStruct((peers //...  16.4 us
    ppermute x3, starting transfers between devices, body(): lax.ppermute(packed, ('energy', 'space'), moves)  4.31 us
    unnamed x11, local copies, waits for them, and re-layouts  3.58 us
    ppermute x3, waiting for transfers between devices, body(): lax.ppermute(packed, ('energy', 'space'), moves)  3.28 us
  transfers between devices with their start and end apart: 4, of which 3 were waited for; matrix products, arithmetic and copies ran while one was open for 0% of the time, Pallas kernels for 0%

profile of v3, /device:TPU:0, one launch (start us, length us, event | category | flops | bytes accessed | tf_op | source)
XLA Modules:
  0.0 48.5 jit_solution(18052208119131041044)
XLA Ops:
  0.0 0.0 copy-start.3
  0.0 0.0 copy-start.4
  0.0 0.0 copy-start.2
  0.0 0.7 %copy-done.3 = f32[1,1,256]{2,1,0:T(1,128)S(1)} copy-done((f32[1,1,256]{2,1,0:T(1,128)S(1)}, f32[1,1,256]{2,1,0:T(1,128)}, u32[]{:S(2)}) %copy-start.3) | copy-done | bytes 1048
  0.7 0.0 copy-done.4
  0.7 0.0 copy-done.2
  0.7 4.1 %collective-permute-start.1 = (f32[3,256]{1,0:T(4,128)S(1)}, f32[3,256]{1,0:T(4,128)S(1)}, u32[]{:S(2)}, u32[]{:S(2)}) collective-permute-start(f32[3,256]{1,0:T(4,128)S(1)} %get-tuple-element.10), channel_id=1, source_target_pairs={{0,8},{1,9},{2,10},{3,11},{4,12},{5,13},{6,14},{7,15},{8,0},{9,1},... | collective-permute-start | bytes 9224 | tf_op jit(solution)/shard_map/ppermute | solution.py:323
  4.8 0.0 collective-permute-start
  4.8 0.2 collective-permute-start.2
  5.0 0.3 collective-permute-start.3
  5.4 0.1 reverse.5
  5.5 0.5 %collective-permute-done = f32[3,256]{1,0:T(4,128)S(1)} collective-permute-done((f32[3,256]{1,0:T(4,128)S(1)}, f32[3,256]{1,0:T(4,128)S(1)}, u32[]{:S(2)}, u32[]{:S(2)}) %collective-permute-start) | collective-permute-done | bytes 3104 | tf_op jit(solution)/shard_map/ppermute | solution.py:323
  6.0 0.4 collective-permute-done.1
  6.4 2.3 %collective-permute-done.2 = f32[3,256]{1,0:T(4,128)S(1)} collective-permute-done((f32[3,256]{1,0:T(4,128)S(1)}, f32[3,256]{1,0:T(4,128)S(1)}, u32[]{:S(2)}, u32[]{:S(2)}) %collective-permute-start.2) | collective-permute-done | bytes 3104 | tf_op jit(solution)/shard_map/ppermute | solution.py:323
  8.8 0.0 collective-permute-done.3.far_ref
  8.8 0.0 copy-start
  8.8 1.0 %copy-done = f32[1,2,256,256]{3,2,1,0:T(8,128)S(1)} copy-done((f32[1,2,256,256]{3,2,1,0:T(8,128)S(1)}, f32[1,2,256,256]{3,2,1,0:T(8,128)}, u32[]{:S(2)}) %copy-start) | copy-done | bytes 524312
  9.8 0.0 copy-start.1
  9.8 1.0 %copy-done.1 = f32[1,2,256,256]{3,2,1,0:T(8,128)S(1)} copy-done((f32[1,2,256,256]{3,2,1,0:T(8,128)S(1)}, f32[1,2,256,256]{3,2,1,0:T(8,128)}, u32[]{:S(2)}) %copy-start.1) | copy-done | bytes 524312
  10.9 20.3 %shard_map.55 = (f32[2,256,512]{2,1,0:T(8,128)S(1)}, f32[2,256,512]{2,1,0:T(8,128)S(1)}) custom-call(f32[2]{0:T(128)S(1)} %broadcast_select_fusion.scal_ref, s32[1]{0:T(128)} %bitcast.9.side_ref, f32[2,256,256]{2,1,0:T(8,128)S(1)} %bitcast.15, f32[2,256,256]{2,1,0:T(8,128)S(1)} %collective-permute-done.3.far_ref, f32[2,256,256]{2,1,0:T(8,128)S(1)} %bitcast.17, ...), custom_call_target="tpu_custom_call" | custom-call | tf_op jit(solution)/shard_map/pallas_call | solution.py:250
  31.2 16.4 %shard_map.56 = f32[8,2,2,16,256]{4,3,2,1,0:T(8,128)S(1)} custom-call(f32[2,2,3,256]{3,2,1,0:T(4,128)S(1)} %reverse_select_fusion.sig_ref, f32[2,256,512]{2,1,0:T(8,128)S(1)} %get-tuple-element.7.green_ref, f32[2,256,512]{2,1,0:T(8,128)S(1)} %get-tuple-element.8.x_ref), custom_call_target="tpu_custom_call" | custom-call | tf_op jit(solution)/shard_map/pallas_call | solution.py:267
  47.7 0.8 %copy.7 = f32[8,2,2,16,256]{4,3,2,1,0:T(8,128)} copy(f32[8,2,2,16,256]{4,3,2,1,0:T(8,128)S(1)} %shard_map.56) | data formatting | bytes 1048576
  (7 shorter events, 0.1 us)
Async XLA Ops:
  0.0 0.7 %copy-start.3 = (f32[1,1,256]{2,1,0:T(1,128)S(1)}, f32[1,1,256]{2,1,0:T(1,128)}, u32[]{:S(2)}) copy-start(f32[1,1,256]{2,1,0:T(1,128)} %param.8) | copy-start | bytes 3076
  0.0 0.7 %copy-start.4 = (f32[1,1,256]{2,1,0:T(1,128)S(1)}, f32[1,1,256]{2,1,0:T(1,128)}, u32[]{:S(2)}) copy-start(f32[1,1,256]{2,1,0:T(1,128)} %param.7) | copy-start | bytes 3076
  0.0 0.7 %copy-start.2 = (f32[1,1,256]{2,1,0:T(1,128)S(1)}, f32[1,1,256]{2,1,0:T(1,128)}, u32[]{:S(2)}) copy-start(f32[1,1,256]{2,1,0:T(1,128)} %param.9) | copy-start | bytes 3076
  0.7 5.7 %collective-permute-start.1 = (f32[3,256]{1,0:T(4,128)S(1)}, f32[3,256]{1,0:T(4,128)S(1)}, u32[]{:S(2)}, u32[]{:S(2)}) collective-permute-start(f32[3,256]{1,0:T(4,128)S(1)} %get-tuple-element.10), channel_id=1, source_target_pairs={{0,8},{1,9},{2,10},{3,11},{4,12},{5,13},{6,14},{7,15},{8,0},{9,1},... | collective-permute-start | bytes 9224 | tf_op jit(solution)/shard_map/ppermute | solution.py:323
  4.8 1.2 %collective-permute-start = (f32[3,256]{1,0:T(4,128)S(1)}, f32[3,256]{1,0:T(4,128)S(1)}, u32[]{:S(2)}, u32[]{:S(2)}) collective-permute-start(f32[3,256]{1,0:T(4,128)S(1)} %get-tuple-element.10), channel_id=1, source_target_pairs={{0,1},{1,0},{2,3},{3,2},{4,5},{5,4},{6,7},{7,6},{8,9},{9,8},{10,11... | collective-permute-start | bytes 9224 | tf_op jit(solution)/shard_map/ppermute | solution.py:323
  4.8 3.9 %collective-permute-start.2 = (f32[3,256]{1,0:T(4,128)S(1)}, f32[3,256]{1,0:T(4,128)S(1)}, u32[]{:S(2)}, u32[]{:S(2)}) collective-permute-start(f32[3,256]{1,0:T(4,128)S(1)} %get-tuple-element.10), channel_id=1, source_target_pairs={{0,9},{1,8},{2,11},{3,10},{4,13},{5,12},{6,15},{7,14},{8,1},{9,0},... | collective-permute-start | bytes 9224 | tf_op jit(solution)/shard_map/ppermute | solution.py:323
  5.0 3.8 %collective-permute-start.3 = (f32[2,256,256]{2,1,0:T(8,128)}, f32[2,256,256]{2,1,0:T(8,128)S(1)}, u32[]{:S(2)}, u32[]{:S(2)}) collective-permute-start(f32[2,256,256]{2,1,0:T(8,128)} %bitcast.16), channel_id=1, source_target_pairs={{0,1},{1,0},{2,3},{3,2},{4,5},{5,4},{6,7},{7,6},{8,9},{9,8},{10,11... | collective-permute-start | bytes 1572872 | tf_op jit(solution)/shard_map/ppermute | solution.py:315
  8.8 1.0 %copy-start = (f32[1,2,256,256]{3,2,1,0:T(8,128)S(1)}, f32[1,2,256,256]{3,2,1,0:T(8,128)}, u32[]{:S(2)}) copy-start(f32[1,2,256,256]{3,2,1,0:T(8,128)} %param.6) | copy-start | bytes 1572868
  9.8 1.0 %copy-start.1 = (f32[1,2,256,256]{3,2,1,0:T(8,128)S(1)}, f32[1,2,256,256]{3,2,1,0:T(8,128)}, u32[]{:S(2)}) copy-start(f32[1,2,256,256]{3,2,1,0:T(8,128)} %param.5) | copy-start | bytes 1572868

commit v4 on v3

--- a/solution.py
+++ b/solution.py
@@ -75,7 +75,9 @@
     bounds = []
     for j in each:
         normal = mul1(a_ref[j], a_ref[j], NT)
-        bounds.append(jnp.sqrt(total(normal)))
+        mean = jnp.sum(normal * eye2(order)) / order
+        spread = jnp.maximum(total(normal) / order - mean * mean, 0.0)
+        bounds.append(1.02 * (mean + jnp.sqrt(spread * (order - 1.0))))
         pair_ref[j, :order] = ah_ref[j] / bounds[j]
         pair_ref[j, order:] = normal / bounds[j]
 
@@ -104,7 +106,7 @@
             for j in each:
                 inverse = pair_ref[j, :order]
                 left = eye2(order) - mul3(a_ref[j], inverse)
-                pair_ref[j, :order] = inverse + mul(inverse, left)
+                pair_ref[j, :order] = inverse + mul(inverse, left + mul(left, left))
                 sizes.append(total(left))
             return state[0] + 1, largest(sizes)
 
@@ -112,12 +114,12 @@
 
     def iterate(mul, limit):
         return lax.while_loop(
-            lambda s: (s[0] < limit) & (s[1] > 4e-6), newton(mul), (jnp.int32(0), F32(1.0))
+            lambda s: (s[0] < limit) & (s[1] > 4e-4), newton(mul), (jnp.int32(0), F32(1.0))
         )[1]
 
     size = iterate(mul1, 5)
 
-    @pl.when(jnp.logical_not(size <= 4e-6))
+    @pl.when(jnp.logical_not(size <= 4e-4))
     def _():
         for j in each:
             pair_ref[j, :order] = ah_ref[j] / bounds[j]

time: 48.7 us -> 47.3 us (0.971)
  Pallas kernels: 36.8 us -> 35.4 us
    pallas_call x1, Pallas kernels: 20.3 us -> 19 us  [green_blocks(): pl.pallas_call(green_kernel, out_shape=[jax.ShapeDtypeStruct(shape, F32)]...]
where the time goes in v4:
time: 47.3 us; the launch traced here: 47.1 us
  Pallas kernels  35.4 us (75%)
  starting transfers between devices  4.61 us (10%)
  local copies, waits for them, and re-layouts  3.68 us (8%)
  waiting for transfers between devices  3.28 us (7%)
    pallas_call x1, Pallas kernels, green_blocks(): pl.pallas_call(green_kernel, out_shape=[jax.ShapeDtypeStruct(shape, F32)]...  19 us
    pallas_call x1, Pallas kernels, exchange(): pl.pallas_call(exchange_kernel, out_shape=jax.ShapeDtypeStruct((peers //...  16.4 us
    ppermute x3, starting transfers between devices, body(): lax.ppermute(packed, ('energy', 'space'), moves)  4.31 us
    unnamed x11, local copies, waits for them, and re-layouts  3.58 us
    ppermute x3, waiting for transfers between devices, body(): lax.ppermute(packed, ('energy', 'space'), moves)  3.28 us
  transfers between devices with their start and end apart: 4, of which 3 were waited for; matrix products, arithmetic and copies ran while one was open for 0% of the time, Pallas kernels for 0%

profile of v4, /device:TPU:0, one launch (start us, length us, event | category | flops | bytes accessed | tf_op | source)
XLA Modules:
  0.0 47.1 jit_solution(5480201773972431054)
XLA Ops:
  0.0 0.0 copy-start.3
  0.0 0.0 copy-start.4
  0.0 0.0 copy-start.2
  0.0 0.7 %copy-done.3 = f32[1,1,256]{2,1,0:T(1,128)S(1)} copy-done((f32[1,1,256]{2,1,0:T(1,128)S(1)}, f32[1,1,256]{2,1,0:T(1,128)}, u32[]{:S(2)}) %copy-start.3) | copy-done | bytes 1048
  0.7 0.0 copy-done.4
  0.7 0.0 copy-done.2
  0.7 4.1 %collective-permute-start.1 = (f32[3,256]{1,0:T(4,128)S(1)}, f32[3,256]{1,0:T(4,128)S(1)}, u32[]{:S(2)}, u32[]{:S(2)}) collective-permute-start(f32[3,256]{1,0:T(4,128)S(1)} %get-tuple-element.10), channel_id=1, source_target_pairs={{0,8},{1,9},{2,10},{3,11},{4,12},{5,13},{6,14},{7,15},{8,0},{9,1},... | collective-permute-start | bytes 9224 | tf_op jit(solution)/shard_map/ppermute | solution.py:325
  4.8 0.0 collective-permute-start
  4.8 0.2 collective-permute-start.2
  5.0 0.3 collective-permute-start.3
  5.4 0.1 reverse.5
  5.5 0.5 %collective-permute-done = f32[3,256]{1,0:T(4,128)S(1)} collective-permute-done((f32[3,256]{1,0:T(4,128)S(1)}, f32[3,256]{1,0:T(4,128)S(1)}, u32[]{:S(2)}, u32[]{:S(2)}) %collective-permute-start) | collective-permute-done | bytes 3104 | tf_op jit(solution)/shard_map/ppermute | solution.py:325
  6.0 0.4 collective-permute-done.1
  6.4 2.3 %collective-permute-done.2 = f32[3,256]{1,0:T(4,128)S(1)} collective-permute-done((f32[3,256]{1,0:T(4,128)S(1)}, f32[3,256]{1,0:T(4,128)S(1)}, u32[]{:S(2)}, u32[]{:S(2)}) %collective-permute-start.2) | collective-permute-done | bytes 3104 | tf_op jit(solution)/shard_map/ppermute | solution.py:325
  8.8 0.0 collective-permute-done.3.far_ref
  8.8 0.0 copy-start
  8.8 1.0 %copy-done = f32[1,2,256,256]{3,2,1,0:T(8,128)S(1)} copy-done((f32[1,2,256,256]{3,2,1,0:T(8,128)S(1)}, f32[1,2,256,256]{3,2,1,0:T(8,128)}, u32[]{:S(2)}) %copy-start) | copy-done | bytes 524312
  9.8 0.0 copy-start.1
  9.8 1.0 %copy-done.1 = f32[1,2,256,256]{3,2,1,0:T(8,128)S(1)} copy-done((f32[1,2,256,256]{3,2,1,0:T(8,128)S(1)}, f32[1,2,256,256]{3,2,1,0:T(8,128)}, u32[]{:S(2)}) %copy-start.1) | copy-done | bytes 524312
  10.9 19.0 %shard_map.55 = (f32[2,256,512]{2,1,0:T(8,128)S(1)}, f32[2,256,512]{2,1,0:T(8,128)S(1)}) custom-call(f32[2]{0:T(128)S(1)} %broadcast_select_fusion.scal_ref, s32[1]{0:T(128)} %bitcast.9.side_ref, f32[2,256,256]{2,1,0:T(8,128)S(1)} %bitcast.15, f32[2,256,256]{2,1,0:T(8,128)S(1)} %collective-permute-done.3.far_ref, f32[2,256,256]{2,1,0:T(8,128)S(1)} %bitcast.17, ...), custom_call_target="tpu_custom_call" | custom-call | tf_op jit(solution)/shard_map/pallas_call | solution.py:252
  29.9 16.4 %shard_map.56 = f32[8,2,2,16,256]{4,3,2,1,0:T(8,128)S(1)} custom-call(f32[2,2,3,256]{3,2,1,0:T(4,128)S(1)} %reverse_select_fusion.sig_ref, f32[2,256,512]{2,1,0:T(8,128)S(1)} %get-tuple-element.7.green_ref, f32[2,256,512]{2,1,0:T(8,128)S(1)} %get-tuple-element.8.x_ref), custom_call_target="tpu_custom_call" | custom-call | tf_op jit(solution)/shard_map/pallas_call | solution.py:269
  46.3 0.8 %copy.7 = f32[8,2,2,16,256]{4,3,2,1,0:T(8,128)} copy(f32[8,2,2,16,256]{4,3,2,1,0:T(8,128)S(1)} %shard_map.56) | data formatting | bytes 1048576
  (7 shorter events, 0.1 us)
Async XLA Ops:
  0.0 0.7 %copy-start.3 = (f32[1,1,256]{2,1,0:T(1,128)S(1)}, f32[1,1,256]{2,1,0:T(1,128)}, u32[]{:S(2)}) copy-start(f32[1,1,256]{2,1,0:T(1,128)} %param.8) | copy-start | bytes 3076
  0.0 0.7 %copy-start.4 = (f32[1,1,256]{2,1,0:T(1,128)S(1)}, f32[1,1,256]{2,1,0:T(1,128)}, u32[]{:S(2)}) copy-start(f32[1,1,256]{2,1,0:T(1,128)} %param.7) | copy-start | bytes 3076
  0.0 0.7 %copy-start.2 = (f32[1,1,256]{2,1,0:T(1,128)S(1)}, f32[1,1,256]{2,1,0:T(1,128)}, u32[]{:S(2)}) copy-start(f32[1,1,256]{2,1,0:T(1,128)} %param.9) | copy-start | bytes 3076
  0.7 5.7 %collective-permute-start.1 = (f32[3,256]{1,0:T(4,128)S(1)}, f32[3,256]{1,0:T(4,128)S(1)}, u32[]{:S(2)}, u32[]{:S(2)}) collective-permute-start(f32[3,256]{1,0:T(4,128)S(1)} %get-tuple-element.10), channel_id=1, source_target_pairs={{0,8},{1,9},{2,10},{3,11},{4,12},{5,13},{6,14},{7,15},{8,0},{9,1},... | collective-permute-start | bytes 9224 | tf_op jit(solution)/shard_map/ppermute | solution.py:325
  4.8 1.2 %collective-permute-start = (f32[3,256]{1,0:T(4,128)S(1)}, f32[3,256]{1,0:T(4,128)S(1)}, u32[]{:S(2)}, u32[]{:S(2)}) collective-permute-start(f32[3,256]{1,0:T(4,128)S(1)} %get-tuple-element.10), channel_id=1, source_target_pairs={{0,1},{1,0},{2,3},{3,2},{4,5},{5,4},{6,7},{7,6},{8,9},{9,8},{10,11... | collective-permute-start | bytes 9224 | tf_op jit(solution)/shard_map/ppermute | solution.py:325
  4.8 3.9 %collective-permute-start.2 = (f32[3,256]{1,0:T(4,128)S(1)}, f32[3,256]{1,0:T(4,128)S(1)}, u32[]{:S(2)}, u32[]{:S(2)}) collective-permute-start(f32[3,256]{1,0:T(4,128)S(1)} %get-tuple-element.10), channel_id=1, source_target_pairs={{0,9},{1,8},{2,11},{3,10},{4,13},{5,12},{6,15},{7,14},{8,1},{9,0},... | collective-permute-start | bytes 9224 | tf_op jit(solution)/shard_map/ppermute | solution.py:325
  5.0 3.8 %collective-permute-start.3 = (f32[2,256,256]{2,1,0:T(8,128)}, f32[2,256,256]{2,1,0:T(8,128)S(1)}, u32[]{:S(2)}, u32[]{:S(2)}) collective-permute-start(f32[2,256,256]{2,1,0:T(8,128)} %bitcast.16), channel_id=1, source_target_pairs={{0,1},{1,0},{2,3},{3,2},{4,5},{5,4},{6,7},{7,6},{8,9},{9,8},{10,11... | collective-permute-start | bytes 1572872 | tf_op jit(solution)/shard_map/ppermute | solution.py:317
  8.8 1.0 %copy-start = (f32[1,2,256,256]{3,2,1,0:T(8,128)S(1)}, f32[1,2,256,256]{3,2,1,0:T(8,128)}, u32[]{:S(2)}) copy-start(f32[1,2,256,256]{3,2,1,0:T(8,128)} %param.6) | copy-start | bytes 1572868
  9.8 1.0 %copy-start.1 = (f32[1,2,256,256]{3,2,1,0:T(8,128)S(1)}, f32[1,2,256,256]{3,2,1,0:T(8,128)}, u32[]{:S(2)}) copy-start(f32[1,2,256,256]{3,2,1,0:T(8,128)} %param.5) | copy-start | bytes 1572868
